TPU v7x, 512 devices: a whole 4x8x8 slice. The times are simulated.
512 devices in a mesh: language: 8 (over y_hi, core), fsdp: 64 (over y_lo, x, z).
Axes of the slice: x: 4, y: 8 (y_hi: 4, y_lo: 2; y = y_hi * 2 + y_lo), z: 8, core: 2. Of those that a mesh axis runs over, the one named last changes fastest.
Arguments:
- hidden: bfloat16 [16, 8192, 5120], P('language', 'fsdp'), may hold values from -60 to 60
- latent_grad: bfloat16 [16, 8192, 64], P('language', 'fsdp'), may hold values from -0.15625 to 0.15625
- lang_ids: int32 [16], P('language'), may hold values from 0 to 15, each once
- old_weights: float32 [16], replicated, may hold values from 0.02 to 0.2
- param: float32 [5120, 64], P('fsdp'), may hold values from -6 to 6
- first_moment: float32 [5120, 64], P('fsdp'), may hold values from -6 to 6
- second_moment: float32 [5120, 64], P('fsdp'), may hold values from 0.25 to 4
Outputs:
- new_param: float32 [5120, 64], P('fsdp')
- new_first: float32 [5120, 64], P('fsdp')
- new_second: float32 [5120, 64], P('fsdp')
- new_logweights: float32 [16], replicated
Inputs may be any that keep to these rules, and one draw needn't show every extreme that they name: `lang_ids`: each id appears in exactly one slot.
All inputs are finite; a program needn't handle non-finite values.
Results may differ from a plain program's by a relative error of at most 0.0003.
Values may be sent and summed in bfloat16 or wider, within the bound.
A program may use at most 64 MiB of HBM per device.

v0:
```python
import jax
import jax.numpy as jnp
from jax import lax
from jax.sharding import PartitionSpec as P

STEP = 100


def log_weights(by_lang, square, old_weights):
    logits = jnp.log(old_weights) + old_weights.shape[0] * (by_lang / (square + 1e-06))
    return logits - jnp.log(jnp.sum(jnp.exp(logits)))


def local(hidden, latent_grad, lang_ids, old_weights, param, first_moment, second_moment):
    langs = old_weights.shape[0]
    slot_grad = lax.psum_scatter(
        jnp.einsum("ltd,ltr->dlr", hidden, latent_grad, preferred_element_type=jnp.float32),
        "fsdp",
        scatter_dimension=0,
        tiled=True,
    )
    onehot = (lang_ids[:, None] == jnp.arange(langs, dtype=jnp.int32)[None, :]).astype(jnp.float32)
    total = lax.psum(jnp.sum(slot_grad, axis=1), "language")
    dots = jnp.einsum("dlr,dr->l", slot_grad, total, precision=lax.Precision.HIGHEST)
    leader = (lax.axis_index("language") == 0).astype(jnp.float32)
    square_part = jnp.sum(total * total) * leader
    by_lang_part = jnp.dot(dots, onehot, precision=lax.Precision.HIGHEST)
    by_lang, square = lax.psum((by_lang_part, square_part), ("language", "fsdp"))
    new_logweights = log_weights(by_lang, square, old_weights)
    weights = jnp.exp(new_logweights)
    slot_weight = jnp.dot(onehot, weights, precision=lax.Precision.HIGHEST)
    local_update = jnp.einsum("l,dlr->dr", slot_weight, slot_grad, precision=lax.Precision.HIGHEST)
    update = lax.psum(local_update, "language")
    new_first = 0.9 * first_moment + 0.1 * update
    new_second = 0.95 * second_moment + 0.05 * update * update
    first_hat = new_first / (1.0 - 0.9**STEP)
    second_hat = new_second / (1.0 - 0.95**STEP)
    new_param = param - 0.02 * (first_hat / (jnp.sqrt(second_hat) + 1e-08) + 0.1 * param)
    return (new_param, new_first, new_second, new_logweights)


def solution(mesh):
    placed = (
        P("language", "fsdp", None),
        P("language", "fsdp", None),
        P("language"),
        P(),
        P("fsdp", None),
        P("fsdp", None),
        P("fsdp", None),
    )
    return jax.shard_map(
        local,
        mesh=mesh,
        in_specs=placed,
        out_specs=(P("fsdp", None), P("fsdp", None), P("fsdp", None), P()),
        check_vma=False,
    )
```

profile of v0, /device:TPU:2, one launch (start us, length us, event | category | flops | bytes accessed | tf_op | source)
XLA Modules:
  0.0 505.8 jit_solution(7632736756905314304)
XLA Ops:
  7.2 0.0 copy-start
  7.2 0.0 reduce-scatter.4.cloned.1.call-start
  7.2 1.7 copy-done
  8.9 2.8 fusion.7
  11.7 3.2 copy.16
  14.9 0.0 copy-start.5
  14.9 0.0 copy-start.4
  14.9 0.0 copy-start.1
  14.9 0.0 copy-start.2
  14.9 0.0 copy-start.3
  14.9 0.0 reduce-scatter.4.cloned.1.call-update
  15.0 310.9 %reduce-scatter.4.cloned.1.call-done = f32[80,128]{1,0:T(8,128)} async-done(((f32[5120,128]{1,0:T(8,128)}), f32[80,128]{1,0:T(8,128)}) %reduce-scatter.4.cloned.1.call-update) | async-done | bytes 40976
  325.9 0.9 copy.17
  326.8 27.2 %psum.28 = f32[80,64]{0,1:T(8,128)S(1)} all-reduce(f32[80,64]{0,1:T(8,128)S(1)} %reduce_sum.27), channel_id=1, replica_groups=mesh['language'=8,'fsdp'=64] {'language'}, use_global_device_ids=true, to_apply=%region_2.0 | all-reduce | flops 5120 | bytes 40960 | tf_op jit(solution)/shard_map/psum | solution.py:23
  354.0 0.6 multiply_reduce_fusion
  354.6 0.7 convolution_bitcast_fusion.2
  355.3 0.0 copy-done.5
  355.3 0.2 convolution_bitcast_fusion.1
  356.1 111.2 %all-reduce = (f32[16]{0:T(128)S(1)}, f32[]{:T(128)}) all-reduce(f32[16]{0:T(128)S(1)} %convolution_bitcast_fusion.1, f32[]{:T(128)S(6)} %mul.45), channel_id=1, replica_groups=mesh['language'=8,'fsdp'=64] {'language','fsdp'}, use_global_device_ids=true, to_apply=%region_3.0 | all-reduce | flops 17 | bytes 136 | tf_op jit(solution)/shard_map/psum | solution.py:28
  468.0 0.0 copy-done.4
  468.0 0.6 exponential_reduce_fusion
  469.3 0.0 copy-start.6
  469.3 0.2 convolution_bitcast_fusion
  469.5 0.4 fusion
  469.9 28.4 %psum.31 = f32[80,64]{0,1:T(8,128)S(1)} all-reduce(f32[80,64]{0,1:T(8,128)S(1)} %bitcast.34), channel_id=1, replica_groups=mesh['language'=8,'fsdp'=64] {'language'}, use_global_device_ids=true, to_apply=%region_7.0 | all-reduce | flops 5120 | bytes 40960 | tf_op jit(solution)/shard_map/psum | solution.py:33
  498.3 0.0 copy-done.1
  498.3 0.0 copy-done.2
  498.3 0.0 copy-done.3
  498.3 0.7 multiply_subtract_fusion
  499.0 0.0 copy-done.6
  (2 shorter events, 0.0 us)
Async XLA Ops:
  7.2 1.7 copy-start
  7.2 318.7 %reduce-scatter.4.cloned.1.call-start = ((), (), s32[]{:S(2)}) async-start(), calls=%async_computation.1 | async-start | bytes 2662400
  14.9 340.3 %copy-start.5 = (s32[2]{0:T(128)S(1)}, s32[2]{0:T(128)}, u32[]{:S(2)}) copy-start(s32[2]{0:T(128)} %param.9) | copy-start | bytes 28
  14.9 453.1 %copy-start.4 = (f32[16]{0:T(128)S(1)}, f32[16]{0:T(128)}, u32[]{:S(2)}) copy-start(f32[16]{0:T(128)} %param.10) | copy-start | bytes 196
  14.9 483.4 %copy-start.1 = (f32[80,64]{0,1:T(8,128)S(1)}, f32[80,64]{0,1:T(8,128)}, u32[]{:S(2)}) copy-start(f32[80,64]{0,1:T(8,128)} %param.11) | copy-start | bytes 61444
  14.9 483.4 %copy-start.2 = (f32[80,64]{0,1:T(8,128)S(1)}, f32[80,64]{0,1:T(8,128)}, u32[]{:S(2)}) copy-start(f32[80,64]{0,1:T(8,128)} %param.12) | copy-start | bytes 61444
  14.9 483.4 %copy-start.3 = (f32[80,64]{0,1:T(8,128)S(1)}, f32[80,64]{0,1:T(8,128)}, u32[]{:S(2)}) copy-start(f32[80,64]{0,1:T(8,128)} %param.13) | copy-start | bytes 61444
  469.3 29.7 %copy-start.6 = (f32[16]{0:T(128)}, f32[16]{0:T(128)S(1)}, u32[]{:S(2)}) copy-start(f32[16]{0:T(128)S(1)} %broadcast_subtract_fusion) | copy-start | bytes 196
Sparse Core Ops, SparseCore 0:
  15.1 310.7 reduce-scatter.3
where the time goes:
time: 506 us
  waiting for transfers between devices  311 us (61%)
  blocking collectives  167 us (33%)
  between operations  16.1 us (3%)
  local copies, waits for them, and re-layouts  5.81 us (1%)
    unnamed x2, waiting for transfers between devices  311 us
    psum x1, blocking collectives, local(): lax.psum((by_lang_part, square_part), ('language', 'fsdp'))  111 us
    psum x1, blocking collectives, local(): update = lax.psum(local_update, 'language')  28.4 us
    psum x1, blocking collectives, local(): total = lax.psum(jnp.sum(slot_grad, axis=1), 'language')  27.2 us
  transfers between devices with their start and end apart: 1, of which 1 were waited for; matrix products, arithmetic and copies ran while one was open for 0% of the time, Pallas kernels for 0%

commit v1 on v0

--- a/solution.py
+++ b/solution.py
@@ -25,7 +25,7 @@
     leader = (lax.axis_index("language") == 0).astype(jnp.float32)
     square_part = jnp.sum(total * total) * leader
     by_lang_part = jnp.dot(dots, onehot, precision=lax.Precision.HIGHEST)
-    by_lang, square = lax.psum((by_lang_part, square_part), ("language", "fsdp"))
+    by_lang, square = lax.psum(lax.psum((by_lang_part, square_part), "fsdp"), "language")
     new_logweights = log_weights(by_lang, square, old_weights)
     weights = jnp.exp(new_logweights)
     slot_weight = jnp.dot(onehot, weights, precision=lax.Precision.HIGHEST)

time: 506 us -> 579 us (1.14)
  the two profiles are of different devices: /device:TPU:2 before, /device:TPU:8 now
where the time goes in v1:
time: 579 us; the launch traced here: 578 us
  waiting for transfers between devices  326 us (56%)
  blocking collectives  224 us (39%)
  between operations  16.1 us (3%)
  local copies, waits for them, and re-layouts  5.81 us (1%)
    unnamed x2, waiting for transfers between devices  326 us
    psum x1, blocking collectives, local(): lax.psum((by_lang_part, square_part), 'fsdp')  154 us
    psum x1, blocking collectives, local(): update = lax.psum(local_update, 'language')  27.9 us
    psum x1, blocking collectives, local(): total = lax.psum(jnp.sum(slot_grad, axis=1), 'language')  27.2 us
    psum x1, blocking collectives, local(): lax.psum(lax.psum((by_lang_part, square_part), 'fsdp'), 'language')  14.8 us
  transfers between devices with their start and end apart: 1, of which 1 were waited for; matrix products, arithmetic and copies ran while one was open for 0% of the time, Pallas kernels for 0%

profile of v1, /device:TPU:8, one launch (start us, length us, event | category | flops | bytes accessed | tf_op | source)
XLA Modules:
  0.0 578.2 jit_solution(17938256195887167453)
XLA Ops:
  7.2 0.0 copy-start
  7.2 0.0 reduce-scatter.4.cloned.1.call-start
  7.2 1.7 copy-done
  8.9 2.8 fusion.7
  11.7 3.2 copy.16
  14.9 0.0 copy-start.5
  14.9 0.0 copy-start.4
  14.9 0.0 copy-start.1
  14.9 0.0 copy-start.2
  14.9 0.0 copy-start.3
  14.9 0.0 reduce-scatter.4.cloned.1.call-update
  15.0 325.9 %reduce-scatter.4.cloned.1.call-done = f32[80,128]{1,0:T(8,128)} async-done(((f32[5120,128]{1,0:T(8,128)}), f32[80,128]{1,0:T(8,128)}) %reduce-scatter.4.cloned.1.call-update) | async-done | bytes 40976
  340.9 0.9 copy.17
  341.8 27.2 %psum.42 = f32[80,64]{0,1:T(8,128)S(1)} all-reduce(f32[80,64]{0,1:T(8,128)S(1)} %reduce_sum.27), channel_id=1, replica_groups=mesh['language'=8,'fsdp'=64] {'language'}, use_global_device_ids=true, to_apply=%region_2.0 | all-reduce | flops 5120 | bytes 40960 | tf_op jit(solution)/shard_map/psum | solution.py:23
  369.0 0.6 multiply_reduce_fusion
  369.6 0.7 convolution_bitcast_fusion.2
  370.3 0.0 copy-done.5
  370.3 0.2 convolution_bitcast_fusion.1
  371.1 154.2 %all-reduce = (f32[16]{0:T(128)S(1)}, f32[]{:T(128)}) all-reduce(f32[16]{0:T(128)S(1)} %convolution_bitcast_fusion.1, f32[]{:T(128)S(6)} %mul.45), channel_id=1, replica_groups=mesh['language'=8,'fsdp'=64] {'fsdp'}, use_global_device_ids=true, to_apply=%region_3.0 | all-reduce | flops 17 | bytes 136 | tf_op jit(solution)/shard_map/psum | solution.py:28
  525.4 14.8 %all-reduce.1 = (f32[16]{0:T(128)S(1)}, f32[]{:T(128)}) all-reduce(f32[16]{0:T(128)S(1)} %get-tuple-element.4, f32[]{:T(128)} %get-tuple-element.5), channel_id=1, replica_groups=mesh['language'=8,'fsdp'=64] {'language'}, use_global_device_ids=true, to_apply=%region_4.0 | all-reduce | flops 17 | bytes 136 | tf_op jit(solution)/shard_map/psum | solution.py:28
  540.9 0.0 copy-done.4
  540.9 0.6 exponential_reduce_fusion
  542.2 0.0 copy-start.6
  542.2 0.2 convolution_bitcast_fusion
  542.4 0.4 fusion
  542.8 27.9 %psum.47 = f32[80,64]{0,1:T(8,128)S(1)} all-reduce(f32[80,64]{0,1:T(8,128)S(1)} %bitcast.34), channel_id=1, replica_groups=mesh['language'=8,'fsdp'=64] {'language'}, use_global_device_ids=true, to_apply=%region_9.0 | all-reduce | flops 5120 | bytes 40960 | tf_op jit(solution)/shard_map/psum | solution.py:33
  570.7 0.0 copy-done.1
  570.7 0.0 copy-done.2
  570.7 0.0 copy-done.3
  570.7 0.7 multiply_subtract_fusion
  571.4 0.0 copy-done.6
  (2 shorter events, 0.0 us)
Async XLA Ops:
  7.2 1.7 copy-start
  7.2 333.7 %reduce-scatter.4.cloned.1.call-start = ((), (), s32[]{:S(2)}) async-start(), calls=%async_computation.1 | async-start | bytes 2662400
  14.9 355.3 %copy-start.5 = (s32[2]{0:T(128)S(1)}, s32[2]{0:T(128)}, u32[]{:S(2)}) copy-start(s32[2]{0:T(128)} %param.9) | copy-start | bytes 28
  14.9 525.9 %copy-start.4 = (f32[16]{0:T(128)S(1)}, f32[16]{0:T(128)}, u32[]{:S(2)}) copy-start(f32[16]{0:T(128)} %param.10) | copy-start | bytes 196
  14.9 555.8 %copy-start.1 = (f32[80,64]{0,1:T(8,128)S(1)}, f32[80,64]{0,1:T(8,128)}, u32[]{:S(2)}) copy-start(f32[80,64]{0,1:T(8,128)} %param.11) | copy-start | bytes 61444
  14.9 555.8 %copy-start.2 = (f32[80,64]{0,1:T(8,128)S(1)}, f32[80,64]{0,1:T(8,128)}, u32[]{:S(2)}) copy-start(f32[80,64]{0,1:T(8,128)} %param.12) | copy-start | bytes 61444
  14.9 555.8 %copy-start.3 = (f32[80,64]{0,1:T(8,128)S(1)}, f32[80,64]{0,1:T(8,128)}, u32[]{:S(2)}) copy-start(f32[80,64]{0,1:T(8,128)} %param.13) | copy-start | bytes 61444
  542.2 29.2 %copy-start.6 = (f32[16]{0:T(128)}, f32[16]{0:T(128)S(1)}, u32[]{:S(2)}) copy-start(f32[16]{0:T(128)S(1)} %broadcast_subtract_fusion) | copy-start | bytes 196
Sparse Core Ops, SparseCore 0:
  15.1 325.7 reduce-scatter.3
